TPU v7x, 32 devices: a whole 2x2x4 slice. The times are simulated.
32 devices in a mesh: grp: 2 (over y), wide: 8 (over z, x), narrow: 2 (over core).
Axes of the slice: x: 2, y: 2, z: 4, core: 2. Of those that a mesh axis runs over, the one named last changes fastest.
Arguments:
- frames: bfloat16 [32, 8192], P(('grp', 'wide')), parts along dimension 0, may hold values from -6 to 6
- gate_weight: bfloat16 [8192, 26624], P('narrow', 'wide'), may hold values from -0.0625 to 0.0625
- up_weight: bfloat16 [8192, 26624], P('narrow', 'wide'), may hold values from -0.0625 to 0.0625
- down_weight: bfloat16 [26624, 8192], P('wide', 'narrow'), may hold values from -0.0546875 to 0.0546875
Outputs:
- mixed: bfloat16 [32, 8192], P(('grp', 'wide'), 'narrow'), parts along dimension 0
There are 2 independent parts, one for each index of `grp`. A program takes and returns all parts, laid end to end along the dimension named above; an argument that names none is the same for every part. Nothing has to cross between parts.
All inputs are finite; a program needn't handle non-finite values.
Results may differ from a plain program's by a relative error of at most 0.0051.
Values may be sent and summed in bfloat16 or wider, within the bound.
A program may use at most 384 MiB of HBM per device.

v0:
```python
import jax
import jax.numpy as jnp
from jax import lax
from jax.sharding import PartitionSpec as P


def on_device(frames, gate_weight, up_weight, down_weight):
    local_units = gate_weight.shape[1]
    half_width = gate_weight.shape[0]
    position = lax.axis_index("narrow")
    my_half = lax.dynamic_slice_in_dim(frames, position * half_width, half_width, 1)
    piece = lax.all_gather(my_half, "wide", axis=0, tiled=True)
    partial_pair = jnp.concatenate(
        [
            jnp.dot(piece, gate_weight, preferred_element_type=jnp.float32),
            jnp.dot(piece, up_weight, preferred_element_type=jnp.float32),
        ],
        axis=1,
    )
    paired = lax.psum(partial_pair, "narrow")
    gate = paired[:, :local_units]
    up_part = paired[:, local_units:]
    hidden = (jax.nn.silu(gate) * up_part).astype(jnp.bfloat16)
    mixed = lax.psum_scatter(
        jnp.dot(hidden, down_weight, preferred_element_type=jnp.float32),
        "wide",
        scatter_dimension=0,
        tiled=True,
    )
    return mixed.astype(jnp.bfloat16)


def solution(mesh):
    placed = (
        P(("grp", "wide"), None),
        P("narrow", "wide"),
        P("narrow", "wide"),
        P("wide", "narrow"),
    )
    return jax.shard_map(
        on_device,
        mesh=mesh,
        in_specs=placed,
        out_specs=P(("grp", "wide"), "narrow"),
        check_vma=False,
    )
```

profile of v0, /device:TPU:0, one launch (start us, length us, event | category | flops | bytes accessed | tf_op | source)
XLA Modules:
  0.0 140.3 jit_solution(9639227936895158140)
XLA Ops:
  6.5 0.0 copy-start
  6.5 0.0 all-reduce.4.cloned.1.call-start
  6.5 0.8 copy-done
  7.3 32.3 %all-gather = bf16[8,2,4096]{2,1,0:T(2,128)(2,1)S(1)} all-gather(bf16[1,2,4096]{2,1,0:T(2,128)(2,1)S(1)} %dynamic-slice_bitcast_fusion), channel_id=1, replica_groups=mesh['grp'=2,'wide'=8,'narrow'=2] {'wide'}, dimensions={0}, use_global_device_ids=true | all-gather | bytes 147456 | tf_op jit(solution)/shard_map/all_gather | solution.py:12
  39.6 0.1 reshape.1
  39.7 0.0 copy-start.1
  39.7 10.6 %fusion.5 = f32[16,3328]{1,0:T(8,128)S(1)} fusion(bf16[16,4096]{1,0:T(8,128)(2,1)S(1)} %reshape.1, bf16[4096,3328]{1,0:T(8,128)(2,1)} %param.5), kind=kOutput, calls=%fused_computation.8 | convolution fusion | flops 436207616 | bytes 27607040 | tf_op jit(solution)/shard_map/dot_general | solution.py:15
  50.3 10.6 %fusion.6 = f32[16,3328]{1,0:T(8,128)S(1)} fusion(bf16[16,4096]{1,0:T(8,128)(2,1)S(1)} %reshape.1, bf16[4096,3328]{1,0:T(8,128)(2,1)} %param.6), kind=kOutput, calls=%fused_computation.9 | convolution fusion | flops 436207616 | bytes 27607040 | tf_op jit(solution)/shard_map/dot_general | solution.py:16
  61.0 0.8 pad_maximum_fusion
  61.7 0.0 all-reduce.4.cloned.1.call-update
  61.8 0.0 copy-done.1
  61.8 0.6 dynamic-slice
  63.0 18.4 %all-reduce.4.cloned.1.call-done = f32[16,6656]{1,0:T(8,128)} async-done(((f32[16,6656]{1,0:T(8,128)}), f32[16,6656]{1,0:T(8,128)}) %all-reduce.4.cloned.1.call-update) | async-done | bytes 426000 | tf_op jit(solution)/shard_map/psum | solution.py:20
  81.4 10.7 %fusion.1 = f32[16,4096]{1,0:T(8,128)S(1)} fusion(bf16[3328,4096]{1,0:T(8,128)(2,1)} %param.7, f32[16,6656]{1,0:T(8,128)} %all-reduce.4.cloned.1.call-done), kind=kOutput, calls=%fused_computation.3 | convolution fusion | flops 436527104 | bytes 27951104 | tf_op jit(solution)/shard_map/dot_general | solution.py:25
  92.1 40.7 %all-reduce.5 = bf16[16,4096]{1,0:T(8,128)(2,1)S(1)} all-reduce(f32[16,4096]{1,0:T(8,128)S(1)} %fusion.1), channel_id=2, replica_groups=mesh['grp'=2,'wide'=8,'narrow'=2] {'wide'}, use_global_device_ids=true, to_apply=%region_1.2.clone | all-reduce | flops 65536 | bytes 393216
  132.8 0.6 dynamic-slice_convert_fusion
  (1 shorter events, 0.0 us)
Async XLA Ops:
  6.5 0.8 copy-start
  6.5 74.9 %all-reduce.4.cloned.1.call-start = ((), (), s32[]{:S(2)}) async-start(), calls=%async_computation | async-start | bytes 851968 | tf_op jit(solution)/shard_map/psum | solution.py:20
  39.7 22.1 %copy-start.1 = (u32[32]{0:T(128)S(1)}, u32[32]{0:T(128)}, u32[]{:S(2)}) copy-start(u32[32]{0:T(128)} %constant.16) | copy-start | bytes 388
Sparse Core Ops, SparseCore 0:
  61.9 19.4 all-reduce.3
where the time goes:
time: 140 us
  blocking collectives  73 us (52%)
  matrix products  32 us (23%)
  waiting for transfers between devices  18.4 us (13%)
  between operations  14.1 us (10%)
  local copies, waits for them, and re-layouts  2.04 us (1%)
    unnamed x1, blocking collectives  40.7 us
    all_gather x1, blocking collectives, on_device(): piece = lax.all_gather(my_half, 'wide', axis=0, tiled=True)  32.3 us
    psum x1, waiting for transfers between devices, on_device(): paired = lax.psum(partial_pair, 'narrow')  18.4 us
    dot_general x1, matrix products, on_device(): jnp.dot(hidden, down_weight, preferred_element_type=jnp.float32)  10.7 us
    dot_general x1, matrix products, on_device(): jnp.dot(piece, gate_weight, preferred_element_type=jnp.float32)  10.6 us
    dot_general x1, matrix products, on_device(): jnp.dot(piece, up_weight, preferred_element_type=jnp.float32)  10.6 us
  transfers between devices with their start and end apart: 1, of which 1 were waited for; matrix products, arithmetic and copies ran while one was open for 0% of the time, Pallas kernels for 0%

commit v1 on v0

v1 whole, which is shorter than its diff:
```python
import functools

import jax
import jax.numpy as jnp
from jax import lax
from jax.experimental import pallas as pl
from jax.experimental.pallas import tpu as pltpu
from jax.sharding import PartitionSpec as P

MESH = pl.DeviceIdType.MESH
F32 = jnp.float32
BF16 = jnp.bfloat16
LANES = 128


def kernel(
    n_grp, n_wide, inner, n_col,
    frames, gate_w, up_w, down_w, out,
    xg, xbuf, gu, dn, part, peer_part, hid, peer_hid, acc, sbuf, rbuf,
    x_local_sem, x_send_sem, fwd_send_sem, x_recv_sem, gu_sem, dn_sem,
    nar_send, nar_recv, hid_send, hid_recv, out_send, out_recv,
):
    g = lax.axis_index("grp")
    w = lax.axis_index("wide")
    n = lax.axis_index("narrow")
    half = gate_w.shape[0]
    units = gate_w.shape[1] // n_grp
    chunks = units // LANES
    cols_half = down_w.shape[1] // n_grp
    cols = cols_half // n_col
    rows = frames.shape[0]
    outer = n_wide // inner
    wo, wi = w // inner, lax.rem(w, inner)
    me = g * n_wide + w
    base = pl.multiple_of(g * units, LANES)
    other = pl.multiple_of((n_grp - 1 - g) * units, LANES)
    my_cols = pl.multiple_of(g * cols_half, LANES)

    def gu_copies(j):
        at = pl.multiple_of(base + j * LANES, LANES)
        return [
            pltpu.make_async_copy(
                m.at[:, pl.ds(at, LANES)], gu.at[j, :, pl.ds(k * LANES, LANES)], gu_sem.at[k, j]
            )
            for k, m in enumerate((gate_w, up_w))
        ]

    def dn_copies(j):
        return [
            pltpu.make_async_copy(
                down_w.at[pl.ds(pl.multiple_of(b + j * LANES, LANES), LANES), pl.ds(my_cols, cols_half)],
                dn.at[j, pl.ds(k * LANES, LANES), :],
                dn_sem.at[k, j],
            )
            for k, b in enumerate((base, other))
        ]

    @pl.loop(0, chunks)
    def _(j):
        for c in gu_copies(j):
            c.start()

    @pl.loop(0, chunks)
    def _(j):
        for c in dn_copies(j):
            c.start()

    barrier = pltpu.get_barrier_semaphore()
    peers = n_grp * n_wide

    def device(s):
        return {"grp": s // n_wide, "wide": lax.rem(s, n_wide), "narrow": n}

    @pl.loop(1, peers)
    def _(d):
        pl.semaphore_signal(barrier, inc=1, device_id=device(lax.rem(me + d, peers)), device_id_type=MESH)

    pl.semaphore_signal(barrier, inc=1, device_id={"narrow": 1 - n}, device_id_type=MESH)
    pl.semaphore_wait(barrier, peers)

    my_x = frames.at[:, pl.ds(pl.multiple_of(n * half, LANES), half)]

    def x_copy(src, s, sem, dev):
        return pltpu.make_async_remote_copy(
            src_ref=src, dst_ref=xg.at[s], send_sem=sem, recv_sem=x_recv_sem.at[s],
            device_id=dev, device_id_type=MESH,
        )

    plane = [(dg, di) for dg in range(n_grp) for di in range(inner) if dg or di]

    def plane_device(dg, di):
        return {
            "grp": lax.rem(g + dg, n_grp),
            "wide": wo * inner + lax.rem(wi + di, inner),
            "narrow": n,
        }

    def outer_slot(d):
        return g * n_wide + lax.rem(wo + d, outer) * inner + wi

    sends = []
    for d in range(1, outer):
        sends.append(x_copy(my_x, me, x_send_sem.at[d - 1], device(outer_slot(d))))
    for k, (dg, di) in enumerate(plane):
        sends.append(x_copy(my_x, me, x_send_sem.at[outer - 1 + k], plane_device(dg, di)))
    for c in sends:
        c.start()
    local = pltpu.make_async_copy(my_x, xg.at[me], x_local_sem)
    local.start()
    for d in range(1, outer):
        s = outer_slot(d)
        x_copy(my_x, s, x_send_sem.at[0], device(s)).wait_recv()
        for k, (dg, di) in enumerate(plane):
            c = x_copy(xg.at[s], s, fwd_send_sem.at[(d - 1) * len(plane) + k], plane_device(dg, di))
            c.start()
            sends.append(c)
    local.wait()
    for dg, di in plane:
        for d in range(outer):
            s = lax.rem(g + dg, n_grp) * n_wide + lax.rem(wo + d, outer) * inner + lax.rem(wi + di, inner)
            x_copy(my_x, s, x_send_sem.at[0], device(s)).wait_recv()
    for s in range(peers):
        xbuf[s * rows : (s + 1) * rows, :] = xg[s]

    def nar_copy(j):
        return pltpu.make_async_remote_copy(
            src_ref=part.at[j], dst_ref=peer_part.at[j], send_sem=nar_send.at[j], recv_sem=nar_recv.at[j],
            device_id={"narrow": 1 - n}, device_id_type=MESH,
        )

    def hid_copy(j):
        return pltpu.make_async_remote_copy(
            src_ref=hid.at[j], dst_ref=peer_hid.at[j], send_sem=hid_send.at[j], recv_sem=hid_recv.at[j],
            device_id={"grp": n_grp - 1 - g}, device_id_type=MESH,
        )

    def project(j):
        for c in gu_copies(j):
            c.wait()
        part[j] = jnp.dot(xbuf[...], gu[j], preferred_element_type=F32)
        nar_copy(j).start()

    def activate(j):
        nar_copy(j).wait_recv()
        both = part[j] + peer_part[j]
        gate, up = both[:, :LANES], both[:, LANES:]
        hid[j] = (gate / (1.0 + jnp.exp(-gate)) * up).astype(BF16)
        hid_copy(j).start()

    project(0)

    @pl.loop(1, chunks)
    def _(j):
        project(j)
        activate(j - 1)

    early = chunks - 2

    def down(c, js):
        total = None
        for j in js:
            lhs = jnp.concatenate([hid[j], peer_hid[j]], axis=1)
            term = jnp.dot(lhs, dn[j, :, c * cols : (c + 1) * cols], preferred_element_type=F32)
            total = term if total is None else total + term
        return total

    for j in range(early):
        hid_copy(j).wait_recv()
        for c in dn_copies(j):
            c.wait()
    acc[0] = down(0, range(early))
    activate(chunks - 1)
    for c in range(1, n_col):
        acc[c] = down(c, range(early))
    for j in range(early, chunks):
        hid_copy(j).wait_recv()
        for c in dn_copies(j):
            c.wait()

    def out_copy(c, d):
        s = lax.rem(me + d, peers)
        return pltpu.make_async_remote_copy(
            src_ref=sbuf.at[c, s], dst_ref=rbuf.at[c, me],
            send_sem=out_send.at[c, d], recv_sem=out_recv.at[c, me],
            device_id=device(s), device_id_type=MESH,
        )

    def out_arrival(c, d):
        s = lax.rem(me + d, peers)
        return pltpu.make_async_remote_copy(
            src_ref=sbuf.at[c, s], dst_ref=rbuf.at[c, s],
            send_sem=out_send.at[c, d], recv_sem=out_recv.at[c, s],
            device_id=device(s), device_id_type=MESH,
        )

    for c in range(n_col):
        total = acc[c] + down(c, range(early, chunks))
        for s in range(peers):
            sbuf[c, s] = total[s * rows : (s + 1) * rows, :].astype(BF16)

        @pl.loop(1, peers)
        def _(d):
            out_copy(c, d).start()

        rbuf[c, me] = sbuf[c, me]

    for c in range(n_col):
        @pl.loop(1, peers)
        def _(d):
            out_arrival(c, d).wait_recv()

        for k in range(n_grp):
            total = rbuf[c, k * n_wide].astype(F32)
            for i in range(1, n_wide):
                total = total + rbuf[c, k * n_wide + i].astype(F32)
            at = k * cols_half + c * cols
            out[:, at : at + cols] = total.astype(BF16)

    for c in sends:
        c.wait_send()

    @pl.loop(0, chunks)
    def _(j):
        nar_copy(j).wait_send()
        hid_copy(j).wait_send()

    for c in range(n_col):
        @pl.loop(1, peers)
        def _(d):
            out_copy(c, d).wait_send()


def fused(n_grp, n_wide, inner, n_col, frames, gate_w, up_w, down_w):
    half = gate_w.shape[0]
    units = gate_w.shape[1] // n_grp
    chunks = units // LANES
    width = down_w.shape[1]
    cols_half = width // n_grp
    cols = cols_half // n_col
    rows = frames.shape[0]
    peers = n_grp * n_wide
    tokens = rows * peers
    outer = n_wide // inner
    plane = n_grp * inner - 1
    dma = pltpu.SemaphoreType.DMA
    return pl.pallas_call(
        functools.partial(kernel, n_grp, n_wide, inner, n_col),
        out_shape=jax.ShapeDtypeStruct((rows, width), BF16),
        in_specs=[pl.BlockSpec(memory_space=pl.ANY)] * 4,
        out_specs=pl.BlockSpec(memory_space=pltpu.VMEM),
        scratch_shapes=[
            pltpu.VMEM((peers, rows, half), BF16),
            pltpu.VMEM((tokens, half), BF16),
            pltpu.VMEM((chunks, half, 2 * LANES), BF16),
            pltpu.VMEM((chunks, 2 * LANES, cols_half), BF16),
            pltpu.VMEM((chunks, tokens, 2 * LANES), F32),
            pltpu.VMEM((chunks, tokens, 2 * LANES), F32),
            pltpu.VMEM((chunks, tokens, LANES), BF16),
            pltpu.VMEM((chunks, tokens, LANES), BF16),
            pltpu.VMEM((n_col, tokens, cols), F32),
            pltpu.VMEM((n_col, peers, rows, cols), BF16),
            pltpu.VMEM((n_col, peers, rows, cols), BF16),
            dma,
            dma((outer - 1 + plane,)),
            dma(((outer - 1) * plane,)),
            dma((peers,)),
            dma((2, chunks)),
            dma((2, chunks)),
            dma((chunks,)),
            dma((chunks,)),
            dma((chunks,)),
            dma((chunks,)),
            dma((n_col, peers)),
            dma((n_col, peers)),
        ],
        compiler_params=pltpu.CompilerParams(
            collective_id=0, has_side_effects=True, vmem_limit_bytes=60 * 1024 * 1024
        ),
        cost_estimate=pl.CostEstimate(
            flops=2 * tokens * 3 * half * units, bytes_accessed=6 * half * units, transcendentals=tokens * units
        ),
    )(frames, gate_w, up_w, down_w)


def plain(frames, gate_weight, up_weight, down_weight):
    local_units = gate_weight.shape[1]
    half_width = gate_weight.shape[0]
    position = lax.axis_index("narrow")
    my_half = lax.dynamic_slice_in_dim(frames, position * half_width, half_width, 1)
    piece = lax.all_gather(my_half, "wide", axis=0, tiled=True)
    partial_pair = jnp.concatenate(
        [
            jnp.dot(piece, gate_weight, preferred_element_type=F32),
            jnp.dot(piece, up_weight, preferred_element_type=F32),
        ],
        axis=1,
    )
    paired = lax.psum(partial_pair, "narrow")
    gate = paired[:, :local_units]
    up_part = paired[:, local_units:]
    hidden = (jax.nn.silu(gate) * up_part).astype(BF16)
    mixed = lax.psum_scatter(
        jnp.dot(hidden, down_weight, preferred_element_type=F32),
        "wide",
        scatter_dimension=0,
        tiled=True,
    )
    return mixed.astype(BF16)


def solution(mesh):
    n_grp, n_wide, n_narrow = (mesh.shape[a] for a in ("grp", "wide", "narrow"))

    def on_device(frames, gate_weight, up_weight, down_weight):
        half, units = gate_weight.shape
        fits = (
            n_grp == 2
            and n_narrow == 2
            and n_wide % 2 == 0
            and n_wide > 2
            and units % (n_grp * LANES) == 0
            and units // (n_grp * LANES) > 2
            and 3 * half * units <= 42 * 1024 * 1024
            and n_grp * n_wide * frames.shape[0] <= 32
        )
        if fits:
            return fused(n_grp, n_wide, 2, 2, frames, gate_weight, up_weight, down_weight)
        return plain(frames, gate_weight, up_weight, down_weight)

    placed = (
        P(("grp", "wide"), None),
        P("narrow", "wide"),
        P("narrow", "wide"),
        P("wide", "narrow"),
    )
    return jax.shard_map(
        on_device,
        mesh=mesh,
        in_specs=placed,
        out_specs=P(("grp", "wide"), "narrow"),
        check_vma=False,
    )
```

time: 140 us -> 42.2 us (0.30)
  blocking collectives: 73 us -> 0 us
  Pallas kernels: 0 us -> 40.6 us
  matrix products: 32 us -> 0 us
  waiting for transfers between devices: 18.4 us -> 0 us
  between operations: 14.1 us -> 0.01 us
    unnamed x1 -> x0, blocking collectives: 40.7 us -> none
    pallas_call x0 -> x1, Pallas kernels: none -> 40.6 us  [fused(): pl.pallas_call(functools.partial(kernel, n_grp, n_wide, inner, n_col), ou...]
    all_gather x1 -> x0, blocking collectives: 32.3 us -> none  [on_device(): piece = lax.all_gather(my_half, 'wide', axis=0, tiled=True)]
    dot_general x3 -> x0, matrix products: 32 us -> none  [the longest x1 10.7 us: on_device(): jnp.dot(hidden, down_weight, preferred_element_type=jnp.float32)]
    psum x1 -> x0, waiting for transfers between devices: 18.4 us -> none  [on_device(): paired = lax.psum(partial_pair, 'narrow')]
  transfers between devices with their start and end apart: 1 -> 0, of which waited for: 1 -> 0; matrix products, arithmetic and copies ran while one was open for 0% -> 0% of each run, Pallas kernels for 0% -> 0%
where the time goes in v1:
time: 42.2 us; the launch traced here: 41.9 us
  Pallas kernels  40.6 us (96%)
  local copies, waits for them, and re-layouts  1.34 us (3%)
    pallas_call x1, Pallas kernels, fused(): pl.pallas_call(functools.partial(kernel, n_grp, n_wide, inner, n_col), ou...  40.6 us
    unnamed x1, local copies, waits for them, and re-layouts  1.34 us

profile of v1, /device:TPU:0, one launch (start us, length us, event | category | flops | bytes accessed | tf_op | source)
XLA Modules:
  0.0 41.9 jit_solution(1181254017103278289)
XLA Ops:
  0.0 40.6 %shard_map.46 = bf16[2,4096]{1,0:T(2,128)(2,1)} custom-call(bf16[2,8192]{1,0:T(2,128)(2,1)} %frames.1, bf16[4096,3328]{1,0:T(8,128)(2,1)} %gate_w.1, bf16[4096,3328]{1,0:T(8,128)(2,1)} %up_w.1, bf16[3328,4096]{1,0:T(8,128)(2,1)} %down_w.1), custom_call_target="tpu_custom_call" | custom-call | flops 1308622848 | bytes 40894464 | tf_op jit(solution)/shard_map/pallas_call | solution.py:246
  40.6 1.3 %copy.6 = bf16[2,4096]{1,0:T(2,128)(2,1)} copy(bf16[2,4096]{1,0:T(2,128)(2,1)} %shard_map.46) | data formatting | bytes 32768

commit v2 on v1

--- a/solution.py
+++ b/solution.py
@@ -11,6 +11,7 @@
 F32 = jnp.float32
 BF16 = jnp.bfloat16
 LANES = 128
+LAG = 3
 
 
 def kernel(
@@ -55,36 +56,11 @@
             for k, b in enumerate((base, other))
         ]
 
-    @pl.loop(0, chunks)
-    def _(j):
-        for c in gu_copies(j):
-            c.start()
-
-    @pl.loop(0, chunks)
-    def _(j):
-        for c in dn_copies(j):
-            c.start()
-
     barrier = pltpu.get_barrier_semaphore()
     peers = n_grp * n_wide
 
     def device(s):
         return {"grp": s // n_wide, "wide": lax.rem(s, n_wide), "narrow": n}
-
-    @pl.loop(1, peers)
-    def _(d):
-        pl.semaphore_signal(barrier, inc=1, device_id=device(lax.rem(me + d, peers)), device_id_type=MESH)
-
-    pl.semaphore_signal(barrier, inc=1, device_id={"narrow": 1 - n}, device_id_type=MESH)
-    pl.semaphore_wait(barrier, peers)
-
-    my_x = frames.at[:, pl.ds(pl.multiple_of(n * half, LANES), half)]
-
-    def x_copy(src, s, sem, dev):
-        return pltpu.make_async_remote_copy(
-            src_ref=src, dst_ref=xg.at[s], send_sem=sem, recv_sem=x_recv_sem.at[s],
-            device_id=dev, device_id_type=MESH,
-        )
 
     plane = [(dg, di) for dg in range(n_grp) for di in range(inner) if dg or di]
 
@@ -97,6 +73,31 @@
 
     def outer_slot(d):
         return g * n_wide + lax.rem(wo + d, outer) * inner + wi
+
+    near = [device(outer_slot(d)) for d in range(1, outer)]
+    near += [plane_device(dg, di) for dg, di in plane] + [{"narrow": 1 - n}]
+    for dev in near:
+        pl.semaphore_signal(barrier, inc=1, device_id=dev, device_id_type=MESH)
+
+    @pl.loop(0, chunks)
+    def _(j):
+        for c in gu_copies(j):
+            c.start()
+
+    @pl.loop(0, chunks)
+    def _(j):
+        for c in dn_copies(j):
+            c.start()
+
+    pl.semaphore_wait(barrier, len(near))
+
+    my_x = frames.at[:, pl.ds(pl.multiple_of(n * half, LANES), half)]
+
+    def x_copy(src, s, sem, dev):
+        return pltpu.make_async_remote_copy(
+            src_ref=src, dst_ref=xg.at[s], send_sem=sem, recv_sem=x_recv_sem.at[s],
+            device_id=dev, device_id_type=MESH,
+        )
 
     sends = []
     for d in range(1, outer):
@@ -147,14 +148,15 @@
         hid[j] = (gate / (1.0 + jnp.exp(-gate)) * up).astype(BF16)
         hid_copy(j).start()
 
-    project(0)
-
-    @pl.loop(1, chunks)
+    for j in range(LAG):
+        project(j)
+
+    @pl.loop(LAG, chunks)
     def _(j):
         project(j)
-        activate(j - 1)
-
-    early = chunks - 2
+        activate(j - LAG)
+
+    early = chunks - LAG - 1
 
     def down(c, js):
         total = None
@@ -169,7 +171,8 @@
         for c in dn_copies(j):
             c.wait()
     acc[0] = down(0, range(early))
-    activate(chunks - 1)
+    for j in range(chunks - LAG, chunks):
+        activate(j)
     for c in range(1, n_col):
         acc[c] = down(c, range(early))
     for j in range(early, chunks):
@@ -319,7 +322,7 @@
             and n_wide % 2 == 0
             and n_wide > 2
             and units % (n_grp * LANES) == 0
-            and units // (n_grp * LANES) > 2
+            and units // (n_grp * LANES) > LAG + 1
             and 3 * half * units <= 42 * 1024 * 1024
             and n_grp * n_wide * frames.shape[0] <= 32
         )

time: 42.2 us -> 39.9 us (0.945)
  Pallas kernels: 40.6 us -> 38.3 us
    pallas_call x1, Pallas kernels: 40.6 us -> 38.3 us  [fused(): pl.pallas_call(functools.partial(kernel, n_grp, n_wide, inner, n_col), ou...]
where the time goes in v2:
time: 39.9 us; the launch traced here: 39.6 us
  Pallas kernels  38.3 us (96%)
  local copies, waits for them, and re-layouts  1.34 us (3%)
    pallas_call x1, Pallas kernels, fused(): pl.pallas_call(functools.partial(kernel, n_grp, n_wide, inner, n_col), ou...  38.3 us
    unnamed x1, local copies, waits for them, and re-layouts  1.34 us

profile of v2, /device:TPU:0, one launch (start us, length us, event | category | flops | bytes accessed | tf_op | source)
XLA Modules:
  0.0 39.6 jit_solution(14122066923929700019)
XLA Ops:
  0.0 38.3 %shard_map.46 = bf16[2,4096]{1,0:T(2,128)(2,1)} custom-call(bf16[2,8192]{1,0:T(2,128)(2,1)} %frames.1, bf16[4096,3328]{1,0:T(8,128)(2,1)} %gate_w.1, bf16[4096,3328]{1,0:T(8,128)(2,1)} %up_w.1, bf16[3328,4096]{1,0:T(8,128)(2,1)} %down_w.1), custom_call_target="tpu_custom_call" | custom-call | flops 1308622848 | bytes 40894464 | tf_op jit(solution)/shard_map/pallas_call | solution.py:249
  38.3 1.3 %copy.6 = bf16[2,4096]{1,0:T(2,128)(2,1)} copy(bf16[2,4096]{1,0:T(2,128)(2,1)} %shard_map.46) | data formatting | bytes 32768

commit v3 on v2

--- a/solution.py
+++ b/solution.py
@@ -166,13 +166,14 @@
             total = term if total is None else total + term
         return total
 
+    for j in range(chunks - LAG, chunks):
+        activate(j)
+
     for j in range(early):
         hid_copy(j).wait_recv()
         for c in dn_copies(j):
             c.wait()
     acc[0] = down(0, range(early))
-    for j in range(chunks - LAG, chunks):
-        activate(j)
     for c in range(1, n_col):
         acc[c] = down(c, range(early))
     for j in range(early, chunks):
@@ -327,7 +328,7 @@
             and n_grp * n_wide * frames.shape[0] <= 32
         )
         if fits:
-            return fused(n_grp, n_wide, 2, 2, frames, gate_weight, up_weight, down_weight)
+            return fused(n_grp, n_wide, 2, 1, frames, gate_weight, up_weight, down_weight)
         return plain(frames, gate_weight, up_weight, down_weight)
 
     placed = (

time: 39.9 us -> 37.2 us (0.932)
  Pallas kernels: 38.3 us -> 35.6 us
    pallas_call x1, Pallas kernels: 38.3 us -> 35.6 us  [fused(): pl.pallas_call(functools.partial(kernel, n_grp, n_wide, inner, n_col), ou...]
where the time goes in v3:
time: 37.2 us; the launch traced here: 36.9 us
  Pallas kernels  35.6 us (96%)
  local copies, waits for them, and re-layouts  1.34 us (4%)
    pallas_call x1, Pallas kernels, fused(): pl.pallas_call(functools.partial(kernel, n_grp, n_wide, inner, n_col), ou...  35.6 us
    unnamed x1, local copies, waits for them, and re-layouts  1.34 us

profile of v3, /device:TPU:0, one launch (start us, length us, event | category | flops | bytes accessed | tf_op | source)
XLA Modules:
  0.0 36.9 jit_solution(6848788523213591371)
XLA Ops:
  0.0 35.6 %shard_map.46 = bf16[2,4096]{1,0:T(2,128)(2,1)} custom-call(bf16[2,8192]{1,0:T(2,128)(2,1)} %frames.1, bf16[4096,3328]{1,0:T(8,128)(2,1)} %gate_w.1, bf16[4096,3328]{1,0:T(8,128)(2,1)} %up_w.1, bf16[3328,4096]{1,0:T(8,128)(2,1)} %down_w.1), custom_call_target="tpu_custom_call" | custom-call | flops 1308622848 | bytes 40894464 | tf_op jit(solution)/shard_map/pallas_call | solution.py:250
  35.6 1.3 %copy.6 = bf16[2,4096]{1,0:T(2,128)(2,1)} copy(bf16[2,4096]{1,0:T(2,128)(2,1)} %shard_map.46) | data formatting | bytes 32768
